TPU v7x, 512 devices: a whole 4x8x8 slice. The times are simulated.
512 devices in a mesh: row: 64 (over y, z_hi, core), col: 8 (over z_lo, x).
Axes of the slice: x: 4, y: 8, z: 8 (z_hi: 4, z_lo: 2; z = z_hi * 2 + z_lo), core: 2. Of those that a mesh axis runs over, the one named last changes fastest.
Arguments:
- grad_out: bfloat16 [256, 32768], P('col', 'row'), may hold values from -0.15917969 to 0.15917969
- pre_act: bfloat16 [256, 32768], P('col', 'row'), may hold values from -6 to 6
- aggregated: bfloat16 [256, 32768], P('col', 'row'), may hold values from -6 to 6
- weight: bfloat16 [256, 256], P(None, 'col'), may hold values from -0.375 to 0.375
- tiles: bfloat16 [6336, 128, 128], P('row'), may hold values from -6 to 6
- tile_coords: int32 [6336, 2], P('row'), may hold values from 0 to 255, as said below
- tile_count: int32 [64], P('row'), may hold values from 8 to 99
Outputs:
- feature_grad: bfloat16 [256, 32768], P('col', 'row')
- weight_grad: float32 [256, 256], P('col')
Inputs may be any that keep to these rules, and one draw needn't show every extreme that they name: `tile_coords`: the block column of every slot of node block b lies within b's own node block (b * 4 to b * 4 + 3). The slots in use are ordered by the node block holding their block row, rising; at most 8 slots in use of one node block have their block rows in one node block, and that many is reached. Slots beyond tile_count hold arbitrary coordinates within the range.
All inputs are finite; a program needn't handle non-finite values.
Results may differ from a plain program's by a relative error of at most 0.011.
Values may be sent and summed in bfloat16 or wider, within the bound.
A program may use at most 64 MiB of HBM per device.

v0:
```python
import jax
import jax.numpy as jnp
from jax import lax
from jax.sharding import PartitionSpec as P

TILE = 128
MAXS = 8


def from_behind(x, axis, by):
    devices = lax.axis_size(axis)
    return lax.ppermute(x, axis, [(i, (i + by) % devices) for i in range(devices)])


def forward(block):
    return from_behind(block, "row", 1)


def shards(grad_out, pre_act, aggregated, weight, tiles, tile_coords, tile_count):
    feat_rows, node_count = grad_out.shape
    blocks_here = node_count // TILE
    slot_count = tiles.shape[0]
    masked = jnp.where(pre_act > 0, grad_out, jnp.zeros_like(grad_out))
    node_grad = lax.psum_scatter(
        jnp.dot(weight, masked, preferred_element_type=jnp.float32),
        "col",
        scatter_dimension=0,
        tiled=True,
    ).astype(jnp.bfloat16)
    local_wgrad = lax.dot_general(
        aggregated,
        lax.all_gather(masked, "col", axis=0, tiled=True),
        (((1,), (1,)), ((), ())),
        preferred_element_type=jnp.float32,
    )
    weight_grad = lax.psum(local_wgrad, "row")
    device = lax.axis_index("row")
    loop_size = lax.axis_size("row")
    block_row = tile_coords[:, 0]
    local_col = tile_coords[:, 1] - device * blocks_here
    in_use = jnp.arange(slot_count, dtype=jnp.int32) < tile_count[0]
    col_onehot = (
        (local_col[:, None] == jnp.arange(blocks_here, dtype=jnp.int32)[None, :]) & in_use[:, None]
    ).astype(jnp.float32)
    source = block_row // blocks_here
    bounds = jnp.arange(loop_size + 1, dtype=jnp.int32)[:, None]
    starts = jnp.sum(((source[None, :] < bounds) & in_use[None, :]).astype(jnp.int32), axis=1)
    slot_lane = jnp.arange(MAXS, dtype=jnp.int32)

    def apply_tiles(totals, block, anchor):
        first_slot = starts[anchor]
        end_slot = starts[anchor + 1]
        picked = first_slot + slot_lane
        is_live = (picked < end_slot).astype(jnp.float32)
        picked = jnp.minimum(picked, slot_count - 1)
        chosen = jnp.take(tiles, picked, axis=0)
        rows_here = jnp.take(block_row, picked) % blocks_here
        block_piece = jnp.take(block.reshape(feat_rows, blocks_here, TILE), rows_here, axis=1)
        products = jnp.einsum(
            "fmi,mij->fmj", block_piece, chosen, preferred_element_type=jnp.float32
        )
        col_weight = jnp.take(col_onehot, picked, axis=0) * is_live[:, None]
        return totals + jnp.einsum("fmj,mb->fbj", products, col_weight)

    totals = jnp.zeros((feat_rows, blocks_here, TILE), jnp.float32)
    totals = apply_tiles(totals, node_grad, device)

    def one_turn(offset, loop_state):
        totals, front_block = loop_state
        front_block = forward(front_block)
        totals = apply_tiles(totals, front_block, (device - offset) % loop_size)
        return (totals, front_block)

    totals, front_block = lax.fori_loop(1, loop_size, one_turn, (totals, node_grad))
    feature_grad = totals.reshape(feat_rows, node_count).astype(jnp.bfloat16)
    return (feature_grad, weight_grad)


def solution(mesh):
    in_specs = (
        P("col", "row"),
        P("col", "row"),
        P("col", "row"),
        P(None, "col"),
        P("row", None, None),
        P("row", None),
        P("row"),
    )
    out_specs = (P("col", "row"), P("col", None))
    return jax.shard_map(shards, mesh=mesh, in_specs=in_specs, out_specs=out_specs, check_vma=False)
```

profile of v0, /device:TPU:1, one launch (start us, length us, event | category | flops | bytes accessed | tf_op | source)
XLA Modules:
  0.0 1044.9 jit_solution(10006126648797113564)
XLA Ops:
  14.2 2.5 gather_fusion.5
  17.4 24.7 %all_gather.3 = bf16[256,512]{1,0:T(8,128)(2,1)S(1)} all-gather(bf16[32,512]{1,0:T(8,128)(2,1)S(1)} %compare_select_fusion.4), channel_id=1, replica_groups=mesh['row'=64,'col'=8] {'col'}, dimensions={0}, use_global_device_ids=true | all-gather | bytes 294912 | tf_op jit(solution)/shard_map/all_gather | solution.py:32
  42.2 280.1 %psum.7 = f32[32,256]{1,0:T(8,128)} all-reduce(f32[32,256]{1,0:T(8,128)S(1)} %convolution_bitcast_fusion.5), channel_id=1, replica_groups=mesh['row'=64,'col'=8] {'row'}, use_global_device_ids=true, to_apply=%region_4.9 | all-reduce | flops 8192 | bytes 65536 | tf_op jit(solution)/shard_map/psum | solution.py:36
  326.6 710.8 %while.19 = (s32[]{:T(128)}, f32[32,4,128]{2,1,0:T(4,128)S(1)}, bf16[32,512]{1,0:T(8,128)(2,1)S(1)}, s32[]{:T(128)}, s32[65]{0:T(128)S(1)}, /*index=5*/bf16[99,1...) while((s32[]{:T(128)}, f32[32,4,128]{2,1,0:T(4,128)S(1)}, ...), condition=%wide.region_3.0_spmd.clone, body=%wide.region_2.7_spmd.clone.sunk | while | flops 8834569 | bytes 1522029 | solution.py:74
  326.6 4.5 collective-permute-start
  335.0 2.5 gather_fusion
  355.3 2.5 gather_fusion
  365.5 2.5 gather_fusion
  386.0 2.5 gather_fusion
  396.8 2.5 gather_fusion
  407.7 2.5 gather_fusion
  418.5 2.5 gather_fusion
  439.9 2.5 gather_fusion
  450.6 2.5 gather_fusion
  461.3 2.5 gather_fusion
  472.0 2.5 gather_fusion
  482.7 2.5 gather_fusion
  504.0 2.5 gather_fusion
  514.7 2.5 gather_fusion
  536.0 2.5 gather_fusion
  546.7 2.5 gather_fusion
  557.3 2.5 gather_fusion
  568.0 2.5 gather_fusion
  578.6 2.5 gather_fusion
  583.5 4.1 collective-permute-start
  591.5 2.5 gather_fusion
  595.9 5.3 collective-permute-start
  605.0 2.5 gather_fusion
  609.4 6.3 collective-permute-start
  619.6 2.5 gather_fusion
  624.0 4.1 collective-permute-start
  636.4 5.1 collective-permute-start
  645.3 2.5 gather_fusion
  649.7 5.9 collective-permute-start
  659.5 2.5 gather_fusion
  663.8 8.4 collective-permute-start
  676.1 2.5 gather_fusion
  686.8 2.5 gather_fusion
  697.5 2.5 gather_fusion
  708.2 2.5 gather_fusion
  718.9 2.5 gather_fusion
  729.6 2.5 gather_fusion
  755.4 2.7 collective-permute-start
  968.4 4.9 collective-permute-start
  981.5 4.1 collective-permute-start
  993.8 5.1 collective-permute-start
  1007.2 5.3 collective-permute-start
  1020.7 8.4 collective-permute-start
  (1121 shorter events, 564.6 us)
Async XLA Ops:
  7.2 317.2 %reduce-scatter.4.cloned.1.call-start = ((), (), s32[]{:S(2)}) async-start(), calls=%async_computation.1 | async-start | bytes 589824
  326.6 11.6 %collective-permute-start = (bf16[32,512]{1,0:T(8,128)(2,1)S(1)}, bf16[32,512]{1,0:T(8,128)(2,1)S(1)}, u32[]{:S(2)}, u32[]{:S(2)}) collective-permute-start(bf16[32,512]{1,0:T(8,128)(2,1)S(1)} %get-tuple-element.468), channel_id=1, source_target_pairs={{0,8},{8,16},{16,24},{24,32},{32,40},{40,48},{48,56},{56,64},{64,7... | collective-permute-start | bytes 98312 | tf_op jit(solution)/shard_map/while/body/eval_jaxpr/ppermute | solution.py:12
  380.2 9.6 collective-permute-start
  391.1 9.6 collective-permute-start
  401.9 9.7 collective-permute-start
  412.7 9.5 collective-permute-start
  423.4 9.5 collective-permute-start
  434.1 9.5 collective-permute-start
  444.8 9.5 collective-permute-start
  455.5 9.5 collective-permute-start
  466.2 9.5 collective-permute-start
  476.9 9.5 collective-permute-start
  487.6 9.5 collective-permute-start
  498.2 9.5 collective-permute-start
  508.9 9.5 collective-permute-start
  519.6 9.5 collective-permute-start
  530.2 9.5 collective-permute-start
  540.9 9.5 collective-permute-start
  551.5 9.5 collective-permute-start
  562.2 9.5 collective-permute-start
  572.9 9.5 collective-permute-start
  583.5 11.1 %collective-permute-start = (bf16[32,512]{1,0:T(8,128)(2,1)S(1)}, bf16[32,512]{1,0:T(8,128)(2,1)S(1)}, u32[]{:S(2)}, u32[]{:S(2)}) collective-permute-start(bf16[32,512]{1,0:T(8,128)(2,1)S(1)} %get-tuple-element.468), channel_id=1, source_target_pairs={{0,8},{8,16},{16,24},{24,32},{32,40},{40,48},{48,56},{56,64},{64,7... | collective-permute-start | bytes 98312 | tf_op jit(solution)/shard_map/while/body/eval_jaxpr/ppermute | solution.py:12
  595.9 12.4 %collective-permute-start = (bf16[32,512]{1,0:T(8,128)(2,1)S(1)}, bf16[32,512]{1,0:T(8,128)(2,1)S(1)}, u32[]{:S(2)}, u32[]{:S(2)}) collective-permute-start(bf16[32,512]{1,0:T(8,128)(2,1)S(1)} %get-tuple-element.468), channel_id=1, source_target_pairs={{0,8},{8,16},{16,24},{24,32},{32,40},{40,48},{48,56},{56,64},{64,7... | collective-permute-start | bytes 98312 | tf_op jit(solution)/shard_map/while/body/eval_jaxpr/ppermute | solution.py:12
  609.4 13.3 %collective-permute-start = (bf16[32,512]{1,0:T(8,128)(2,1)S(1)}, bf16[32,512]{1,0:T(8,128)(2,1)S(1)}, u32[]{:S(2)}, u32[]{:S(2)}) collective-permute-start(bf16[32,512]{1,0:T(8,128)(2,1)S(1)} %get-tuple-element.468), channel_id=1, source_target_pairs={{0,8},{8,16},{16,24},{24,32},{32,40},{40,48},{48,56},{56,64},{64,7... | collective-permute-start | bytes 98312 | tf_op jit(solution)/shard_map/while/body/eval_jaxpr/ppermute | solution.py:12
  624.0 11.2 %collective-permute-start = (bf16[32,512]{1,0:T(8,128)(2,1)S(1)}, bf16[32,512]{1,0:T(8,128)(2,1)S(1)}, u32[]{:S(2)}, u32[]{:S(2)}) collective-permute-start(bf16[32,512]{1,0:T(8,128)(2,1)S(1)} %get-tuple-element.468), channel_id=1, source_target_pairs={{0,8},{8,16},{16,24},{24,32},{32,40},{40,48},{48,56},{56,64},{64,7... | collective-permute-start | bytes 98312 | tf_op jit(solution)/shard_map/while/body/eval_jaxpr/ppermute | solution.py:12
  636.4 12.1 %collective-permute-start = (bf16[32,512]{1,0:T(8,128)(2,1)S(1)}, bf16[32,512]{1,0:T(8,128)(2,1)S(1)}, u32[]{:S(2)}, u32[]{:S(2)}) collective-permute-start(bf16[32,512]{1,0:T(8,128)(2,1)S(1)} %get-tuple-element.468), channel_id=1, source_target_pairs={{0,8},{8,16},{16,24},{24,32},{32,40},{40,48},{48,56},{56,64},{64,7... | collective-permute-start | bytes 98312 | tf_op jit(solution)/shard_map/while/body/eval_jaxpr/ppermute | solution.py:12
  649.7 13.0 %collective-permute-start = (bf16[32,512]{1,0:T(8,128)(2,1)S(1)}, bf16[32,512]{1,0:T(8,128)(2,1)S(1)}, u32[]{:S(2)}, u32[]{:S(2)}) collective-permute-start(bf16[32,512]{1,0:T(8,128)(2,1)S(1)} %get-tuple-element.468), channel_id=1, source_target_pairs={{0,8},{8,16},{16,24},{24,32},{32,40},{40,48},{48,56},{56,64},{64,7... | collective-permute-start | bytes 98312 | tf_op jit(solution)/shard_map/while/body/eval_jaxpr/ppermute | solution.py:12
  663.8 15.5 %collective-permute-start = (bf16[32,512]{1,0:T(8,128)(2,1)S(1)}, bf16[32,512]{1,0:T(8,128)(2,1)S(1)}, u32[]{:S(2)}, u32[]{:S(2)}) collective-permute-start(bf16[32,512]{1,0:T(8,128)(2,1)S(1)} %get-tuple-element.468), channel_id=1, source_target_pairs={{0,8},{8,16},{16,24},{24,32},{32,40},{40,48},{48,56},{56,64},{64,7... | collective-permute-start | bytes 98312 | tf_op jit(solution)/shard_map/while/body/eval_jaxpr/ppermute | solution.py:12
  680.5 9.5 collective-permute-start
  691.2 9.5 collective-permute-start
  701.9 9.5 collective-permute-start
  712.6 9.5 collective-permute-start
  723.3 9.5 collective-permute-start
  734.0 9.5 collective-permute-start
  744.7 9.5 collective-permute-start
  755.4 9.7 collective-permute-start
  766.3 9.4 collective-permute-start
  787.6 9.4 collective-permute-start
  819.5 9.4 collective-permute-start
  851.4 9.4 collective-permute-start
  893.9 9.4 collective-permute-start
  915.1 9.4 collective-permute-start
  925.8 9.5 collective-permute-start
  968.4 11.9 %collective-permute-start = (bf16[32,512]{1,0:T(8,128)(2,1)S(1)}, bf16[32,512]{1,0:T(8,128)(2,1)S(1)}, u32[]{:S(2)}, u32[]{:S(2)}) collective-permute-start(bf16[32,512]{1,0:T(8,128)(2,1)S(1)} %get-tuple-element.468), channel_id=1, source_target_pairs={{0,8},{8,16},{16,24},{24,32},{32,40},{40,48},{48,56},{56,64},{64,7... | collective-permute-start | bytes 98312 | tf_op jit(solution)/shard_map/while/body/eval_jaxpr/ppermute | solution.py:12
  981.5 11.2 %collective-permute-start = (bf16[32,512]{1,0:T(8,128)(2,1)S(1)}, bf16[32,512]{1,0:T(8,128)(2,1)S(1)}, u32[]{:S(2)}, u32[]{:S(2)}) collective-permute-start(bf16[32,512]{1,0:T(8,128)(2,1)S(1)} %get-tuple-element.468), channel_id=1, source_target_pairs={{0,8},{8,16},{16,24},{24,32},{32,40},{40,48},{48,56},{56,64},{64,7... | collective-permute-start | bytes 98312 | tf_op jit(solution)/shard_map/while/body/eval_jaxpr/ppermute | solution.py:12
  993.8 12.1 %collective-permute-start = (bf16[32,512]{1,0:T(8,128)(2,1)S(1)}, bf16[32,512]{1,0:T(8,128)(2,1)S(1)}, u32[]{:S(2)}, u32[]{:S(2)}) collective-permute-start(bf16[32,512]{1,0:T(8,128)(2,1)S(1)} %get-tuple-element.468), channel_id=1, source_target_pairs={{0,8},{8,16},{16,24},{24,32},{32,40},{40,48},{48,56},{56,64},{64,7... | collective-permute-start | bytes 98312 | tf_op jit(solution)/shard_map/while/body/eval_jaxpr/ppermute | solution.py:12
  1007.2 12.4 %collective-permute-start = (bf16[32,512]{1,0:T(8,128)(2,1)S(1)}, bf16[32,512]{1,0:T(8,128)(2,1)S(1)}, u32[]{:S(2)}, u32[]{:S(2)}) collective-permute-start(bf16[32,512]{1,0:T(8,128)(2,1)S(1)} %get-tuple-element.468), channel_id=1, source_target_pairs={{0,8},{8,16},{16,24},{24,32},{32,40},{40,48},{48,56},{56,64},{64,7... | collective-permute-start | bytes 98312 | tf_op jit(solution)/shard_map/while/body/eval_jaxpr/ppermute | solution.py:12
  1020.7 15.5 %collective-permute-start = (bf16[32,512]{1,0:T(8,128)(2,1)S(1)}, bf16[32,512]{1,0:T(8,128)(2,1)S(1)}, u32[]{:S(2)}, u32[]{:S(2)}) collective-permute-start(bf16[32,512]{1,0:T(8,128)(2,1)S(1)} %get-tuple-element.468), channel_id=1, source_target_pairs={{0,8},{8,16},{16,24},{24,32},{32,40},{40,48},{48,56},{56,64},{64,7... | collective-permute-start | bytes 98312 | tf_op jit(solution)/shard_map/while/body/eval_jaxpr/ppermute | solution.py:12
  (17 other events, 184.3 us)
Sparse Core Ops, SparseCore 0:
  10.8 44.0 reduce-scatter.3
where the time goes:
time: 1050 us; the launch traced here: 1040 us
  local copies, waits for them, and re-layouts  324 us (31%)
  blocking collectives  305 us (29%)
  starting transfers between devices  181 us (17%)
  other arithmetic  163 us (16%)
  matrix products  37.4 us (4%)
  between operations  14.8 us (1%)
  waiting for transfers between devices  10.9 us (1%)
    psum x1, blocking collectives, shards(): weight_grad = lax.psum(local_wgrad, 'row')  280 us
    ppermute x63, starting transfers between devices, from_behind(): lax.ppermute(x, axis, [(i, (i + by) % devices) for i in range(devices)])  181 us
    gather x64, local copies, waits for them, and re-layouts, apply_tiles(): chosen = jnp.take(tiles, picked, axis=0)  161 us
    convert_element_type x63, other arithmetic, apply_tiles(): is_live = (picked < end_slot).astype(jnp.float32)  77.3 us
    gather x64, local copies, waits for them, and re-layouts, apply_tiles(): rows_here = jnp.take(block_row, picked) % blocks_here  41.2 us
    and x64, other arithmetic, apply_tiles(): jnp.take(block.reshape(feat_rows, blocks_here, TILE), rows_here, axis=1)  41.1 us
    select_n x64, other arithmetic, apply_tiles(): col_weight = jnp.take(col_onehot, picked, axis=0) * is_live[:, None]  39.8 us
    dynamic_slice x64, local copies, waits for them, and re-layouts, apply_tiles(): end_slot = starts[anchor + 1]  39.7 us
  transfers between devices with their start and end apart: 64, of which 20 were waited for; matrix products, arithmetic and copies ran while one was open for 43% of the time, Pallas kernels for 0%

commit v1 on v0

v1 whole, which is shorter than its diff:
```python
import jax
import jax.numpy as jnp
from jax import lax
from jax.experimental import pallas as pl
from jax.experimental.pallas import tpu as pltpu
from jax.sharding import PartitionSpec as P

YN, ZN, CORES, COLS = 8, 4, 2, 8
WN = ZN * CORES
ROWS = YN * WN
TILE = 128
BLOCKS = 4
FEAT = 32
NODES = BLOCKS * TILE
SLOTS = 99
MESH = pl.DeviceIdType.MESH
ZORDER = (0, 1, 3, 2)


def kernel(
    go_hbm, pa_hbm, agg_hbm, wt_hbm, tiles_hbm, coords_hbm, count_hbm,
    fg_out, wg_out,
    go, pa, agg, wt, tiles, coords, count,
    masked, wpart, wrow, x, wl, ra, part, rb, final,
    in_sem, m_send, m_recv, w_send, w_recv, z_send, z_recv,
    y_send, y_recv, s_send, s_recv, a_send, a_recv, b_send, b_recv, c_send, c_recv,
):
    row = lax.axis_index("row")
    col = lax.axis_index("col")
    y = row // WN
    w = row % WN
    z = w // CORES
    core = w % CORES
    sibling = row + 1 - 2 * core

    def at_col(o):
        return {"row": row, "col": (col + o) % COLS}

    def at_row(r):
        return {"row": r, "col": col}

    def y_row(o):
        return ((y + o) % YN) * WN + w

    def w_row(o):
        return y * WN + (w + o) % WN

    def z_row(o):
        return y * WN + ((z + o) % ZN) * CORES + core

    barrier = pltpu.get_barrier_semaphore()
    for o in range(1, COLS):
        pl.semaphore_signal(barrier, inc=1, device_id=at_col(o), device_id_type=MESH)
    for o in range(1, YN):
        pl.semaphore_signal(barrier, inc=1, device_id=at_row(y_row(o)), device_id_type=MESH)
    for o in range(1, WN):
        pl.semaphore_signal(barrier, inc=1, device_id=at_row(w_row(o)), device_id_type=MESH)

    loads = [
        pltpu.make_async_copy(src, dst, in_sem.at[n])
        for n, (src, dst) in enumerate((
            (go_hbm, go), (pa_hbm, pa), (wt_hbm, wt), (agg_hbm, agg),
            (coords_hbm, coords), (count_hbm, count), (tiles_hbm, tiles),
        ))
    ]
    for load in loads:
        load.start()
    loads[0].wait()
    loads[1].wait()
    masked[col] = jnp.where(pa[...] > 0, go[...], jnp.zeros_like(go[...]))
    loads[2].wait()
    wpart[col] = wt[:, pl.ds(pl.multiple_of((col // 4) * TILE, TILE), TILE)]

    pl.semaphore_wait(barrier, COLS - 1 + YN - 1 + WN - 1)

    def remote(src, dst, send, recv, to):
        return pltpu.make_async_remote_copy(
            src_ref=src, dst_ref=dst, send_sem=send, recv_sem=recv,
            device_id=to, device_id_type=MESH,
        )

    sends = []

    def send(src, dst, send_sem, recv_sem, to):
        copy = remote(src, dst, send_sem, recv_sem, to)
        copy.start()
        sends.append(copy)

    for o in range(1, COLS):
        peer = (col + o) % COLS
        send(
            wt.at[:, pl.ds(pl.multiple_of((peer // 4) * TILE, TILE), TILE)],
            wpart.at[col], w_send.at[o], w_recv.at[COLS - o], at_col(o),
        )
        send(masked.at[col], masked.at[col], m_send.at[o], m_recv.at[COLS - o], at_col(o))
    for o in range(1, COLS):
        peer = (col + o) % COLS
        remote(wpart.at[peer], wpart.at[peer], w_send.at[o], w_recv.at[o], at_col(o)).wait_recv()
    wrow[...] = wpart[...].reshape(COLS * FEAT, TILE).astype(jnp.float32).T
    own_w = wrow[pl.ds(pl.multiple_of((col % 4) * FEAT, FEAT), FEAT), :].astype(jnp.bfloat16)
    for o in range(1, COLS):
        peer = (col + o) % COLS
        remote(masked.at[peer], masked.at[peer], m_send.at[o], m_recv.at[o], at_col(o)).wait_recv()

    m_all = masked[...].reshape(COLS * FEAT, NODES)
    node_grad = jnp.dot(own_w, m_all, preferred_element_type=jnp.float32).astype(jnp.bfloat16)
    for b in range(BLOCKS):
        x[row * BLOCKS + b] = node_grad[:, b * TILE:(b + 1) * TILE]

    def block(r):
        return x.at[pl.ds(r * BLOCKS, BLOCKS)]

    def to_y(step, d, k, r):
        send(block(r), block(r), y_send.at[step, k, d], y_recv.at[step, k + 1, d],
             at_row(y_row(1 - 2 * step)))

    def to_sibling(step, d, k, r):
        send(block(r), block(r), s_send.at[step, k, d], s_recv.at[step, k, d], at_row(sibling))

    def source(step, d, k):
        return ((y - (1 - 2 * step) * k) % YN) * WN + ((z + d) % ZN) * CORES + core

    own = block(row)
    to_y(0, 0, 0, row)
    to_y(1, 0, 0, row)
    for d in (1, 3, 2):
        send(own, own, z_send.at[d], z_recv.at[ZN - d], at_row(z_row(d)))
    to_sibling(0, 0, 0, row)

    loads[3].wait()
    wgrad = lax.dot_general(
        agg[...], m_all, (((1,), (1,)), ((), ())), preferred_element_type=jnp.float32
    )
    for q in range(YN):
        piece = wgrad[(q // 2) * 8:(q // 2) * 8 + 8, (q % 2) * TILE:(q % 2 + 1) * TILE]
        wl[q] = piece
    ra[y] = wl[y]
    for o in range(1, YN):
        send(wl.at[(y + o) % YN], ra.at[y], a_send.at[o], a_recv.at[YN - o], at_row(y_row(o)))

    for d in ZORDER[1:]:
        r = z_row(d)
        remote(block(r), block(r), z_send.at[d], z_recv.at[d], at_row(r)).wait_recv()
        to_y(0, d, 0, r)
        to_y(1, d, 0, r)
        to_sibling(0, d, 0, r)

    def last_leg(step, d):
        return d in ((0, 1) if step == 0 else (3, 2))

    def level(k):
        for d in ZORDER:
            for step in range(2):
                if k == YN // 2 and not last_leg(step, d):
                    continue
                r = source(step, d, k)
                remote(block(r), block(r), y_send.at[step, k, d], y_recv.at[step, k, d],
                       at_row(y_row(1))).wait_recv()
                if k < YN // 2 - 1 or (k == YN // 2 - 1 and last_leg(step, d)):
                    to_y(step, d, k, r)
                to_sibling(step, d, k, r)

    level(1)

    for o in range(1, YN):
        other = (y + o) % YN
        remote(ra.at[other], ra.at[other], a_send.at[o], a_recv.at[o], at_row(y_row(o))).wait_recv()
    part[...] = jnp.sum(ra[...], axis=0)
    rb[w] = part[...]
    for o in range(1, WN):
        send(part, rb.at[w], b_send.at[o], b_recv.at[WN - o], at_row(w_row(o)))

    level(2)

    for o in range(1, WN):
        other = (w + o) % WN
        remote(rb.at[other], rb.at[other], b_send.at[o], b_recv.at[o], at_row(w_row(o))).wait_recv()
    final[y] = jnp.sum(rb[...], axis=0)
    for o in range(1, YN):
        send(final.at[y], final.at[y], c_send.at[o], c_recv.at[YN - o], at_row(y_row(o)))

    level(3)
    level(4)

    for o in range(1, YN):
        other = (y + o) % YN
        remote(final.at[other], final.at[other], c_send.at[o], c_recv.at[o], at_row(y_row(o))).wait_recv()
    for q in range(YN):
        wg_out[(q // 2) * 8:(q // 2) * 8 + 8, (q % 2) * TILE:(q % 2 + 1) * TILE] = final[q]

    for k in range(YN // 2 + 1):
        for d in ZORDER:
            for step in range(1 if k == 0 else 2):
                if k == YN // 2 and not last_leg(step, d):
                    continue
                r = source(step, d, k) + 1 - 2 * core
                remote(block(r), block(r), s_send.at[step, k, d], s_recv.at[step, k, d],
                       at_row(sibling)).wait_recv()

    for load in loads[4:]:
        load.wait()
    in_use = count[0]
    first = row * BLOCKS
    group = 11
    total = jnp.zeros((BLOCKS * FEAT, TILE), jnp.float32)
    for g in range(0, SLOTS, group):
        pieces = []
        for t in range(g, g + group):
            here = x[coords[0, t]]
            j = jnp.where(t < in_use, coords[1, t] - first, -1)
            zero = jnp.zeros_like(here)
            pieces.append(jnp.concatenate(
                [jnp.where(j == b, here, zero) for b in range(BLOCKS)], axis=0))
        total += jnp.dot(
            jnp.concatenate(pieces, axis=1),
            tiles[g:g + group].reshape(group * TILE, TILE),
            preferred_element_type=jnp.float32,
        )
    for b in range(BLOCKS):
        fg_out[:, b * TILE:(b + 1) * TILE] = total[b * FEAT:(b + 1) * FEAT].astype(jnp.bfloat16)

    for copy in sends:
        copy.wait_send()


def shards(grad_out, pre_act, aggregated, weight, tiles, tile_coords, tile_count):
    bf16, f32 = jnp.bfloat16, jnp.float32
    vmem, dma = pltpu.VMEM, pltpu.SemaphoreType.DMA
    return pl.pallas_call(
        kernel,
        out_shape=(
            jax.ShapeDtypeStruct((FEAT, NODES), bf16),
            jax.ShapeDtypeStruct((FEAT, COLS * FEAT), f32),
        ),
        in_specs=[pl.BlockSpec(memory_space=pl.ANY)] * 7,
        out_specs=(pl.BlockSpec(memory_space=vmem), pl.BlockSpec(memory_space=vmem)),
        scratch_shapes=[
            vmem((FEAT, NODES), bf16),
            vmem((FEAT, NODES), bf16),
            vmem((FEAT, NODES), bf16),
            vmem((FEAT, COLS * FEAT), bf16),
            vmem((SLOTS, TILE, TILE), bf16),
            pltpu.SMEM((2, SLOTS), jnp.int32),
            pltpu.SMEM((1,), jnp.int32),
            vmem((COLS, FEAT, NODES), bf16),
            vmem((COLS, FEAT, TILE), bf16),
            vmem((TILE, COLS * FEAT), f32),
            vmem((ROWS * BLOCKS, FEAT, TILE), bf16),
            vmem((YN, 8, TILE), f32),
            vmem((YN, 8, TILE), f32),
            vmem((8, TILE), f32),
            vmem((WN, 8, TILE), f32),
            vmem((YN, 8, TILE), f32),
            dma((7,)),
            dma((COLS,)), dma((COLS,)), dma((COLS,)), dma((COLS,)),
            dma((ZN,)), dma((ZN,)),
            dma((2, 5, ZN)), dma((2, 5, ZN)),
            dma((2, 5, ZN)), dma((2, 5, ZN)),
            dma((YN,)), dma((YN,)), dma((WN,)), dma((WN,)), dma((YN,)), dma((YN,)),
        ],
        compiler_params=pltpu.CompilerParams(
            collective_id=0, has_side_effects=True, vmem_limit_bytes=32 * 1024 * 1024,
        ),
        cost_estimate=pl.CostEstimate(flops=300_000_000, bytes_accessed=6_000_000, transcendentals=0),
    )(grad_out, pre_act, aggregated, weight.T, tiles, tile_coords.T, tile_count)


def solution(mesh):
    in_specs = (
        P("col", "row"),
        P("col", "row"),
        P("col", "row"),
        P(None, "col"),
        P("row", None, None),
        P("row", None),
        P("row"),
    )
    out_specs = (P("col", "row"), P("col", None))
    return jax.shard_map(shards, mesh=mesh, in_specs=in_specs, out_specs=out_specs, check_vma=False)
```

time: 1050 us -> 53.7 us (0.05)
  local copies, waits for them, and re-layouts: 324 us -> 6.81 us
  blocking collectives: 305 us -> 0 us
  starting transfers between devices: 181 us -> 0 us
  other arithmetic: 163 us -> 0 us
  Pallas kernels: 0 us -> 45.1 us
  matrix products: 37.4 us -> 0 us
  between operations: 14.8 us -> 1.3 us
  waiting for transfers between devices: 10.9 us -> 0 us
    psum x1 -> x0, blocking collectives: 280 us -> none  [shards(): weight_grad = lax.psum(local_wgrad, 'row')]
    gather x256 -> x0, local copies, waits for them, and re-layouts: 274 us -> none  [the longest x64 161 us: apply_tiles(): chosen = jnp.take(tiles, picked, axis=0)]
    ppermute x63 -> x0, starting transfers between devices: 181 us -> none  [from_behind(): lax.ppermute(x, axis, [(i, (i + by) % devices) for i in range(devices)])]
    convert_element_type x128 -> x0, other arithmetic: 77.8 us -> none  [the longest x63 77.3 us: apply_tiles(): is_live = (picked < end_slot).astype(jnp.float32)]
    pallas_call x0 -> x1, Pallas kernels: none -> 45.1 us  [shards(): pl.pallas_call(kernel, out_shape=(jax.ShapeDtypeStruct((FEAT, NODES), bf1...]
    and x65 -> x0, other arithmetic: 42.4 us -> none  [the longest x64 41.1 us: apply_tiles(): jnp.take(block.reshape(feat_rows, blocks_here, TILE), rows_here, axis=1)]
    select_n x66 -> x0, other arithmetic: 41.3 us -> none  [the longest x64 39.8 us: apply_tiles(): col_weight = jnp.take(col_onehot, picked, axis=0) * is_live[:, None]]
    dynamic_slice x64 -> x0, local copies, waits for them, and re-layouts: 39.7 us -> none  [apply_tiles(): end_slot = starts[anchor + 1]]
  transfers between devices with their start and end apart: 64 -> 0, of which waited for: 20 -> 0; matrix products, arithmetic and copies ran while one was open for 43% -> 0% of each run, Pallas kernels for 0% -> 0%
where the time goes in v1:
time: 53.7 us; the launch traced here: 53.2 us
  Pallas kernels  45.1 us (84%)
  local copies, waits for them, and re-layouts  6.81 us (13%)
  between operations  1.3 us (2%)
    pallas_call x1, Pallas kernels, shards(): pl.pallas_call(kernel, out_shape=(jax.ShapeDtypeStruct((FEAT, NODES), bf1...  45.1 us
    unnamed x14, local copies, waits for them, and re-layouts  6.81 us

profile of v1, /device:TPU:1, one launch (start us, length us, event | category | flops | bytes accessed | tf_op | source)
XLA Modules:
  0.0 53.2 jit_solution(3789967511870955328)
XLA Ops:
  1.3 0.0 copy-start
  1.3 1.9 %copy-done = bf16[99,128,128]{2,1,0:T(8,128)(2,1)S(1)} copy-done((bf16[99,128,128]{2,1,0:T(8,128)(2,1)S(1)}, bf16[99,128,128]{2,1,0:T(8,128)(2,1)}, u32[]{:S(2)}) %copy-start) | copy-done | bytes 3244056
  3.2 0.0 copy-start.1
  3.2 0.8 %copy-done.1 = bf16[32,512]{1,0:T(8,128)(2,1)S(1)} copy-done((bf16[32,512]{1,0:T(8,128)(2,1)S(1)}, bf16[32,512]{1,0:T(8,128)(2,1)}, u32[]{:S(2)}) %copy-start.1) | copy-done | bytes 32792
  4.0 0.0 copy-start.2
  4.0 0.8 %copy-done.2 = bf16[32,512]{1,0:T(8,128)(2,1)S(1)} copy-done((bf16[32,512]{1,0:T(8,128)(2,1)S(1)}, bf16[32,512]{1,0:T(8,128)(2,1)}, u32[]{:S(2)}) %copy-start.2) | copy-done | bytes 32792
  4.7 0.0 copy-start.3
  4.7 0.8 %copy-done.3 = bf16[32,512]{1,0:T(8,128)(2,1)S(1)} copy-done((bf16[32,512]{1,0:T(8,128)(2,1)S(1)}, bf16[32,512]{1,0:T(8,128)(2,1)}, u32[]{:S(2)}) %copy-start.3) | copy-done | bytes 32792
  5.5 0.0 copy-start.4
  5.5 0.7 %copy-done.4 = bf16[256,32]{0,1:T(8,128)(2,1)S(1)} copy-done((bf16[256,32]{0,1:T(8,128)(2,1)S(1)}, bf16[256,32]{0,1:T(8,128)(2,1)}, u32[]{:S(2)}) %copy-start.4) | copy-done | bytes 16408
  6.2 0.0 copy-start.5
  6.2 0.7 %copy-done.5 = s32[99,2]{0,1:T(2,128)S(1)} copy-done((s32[99,2]{0,1:T(2,128)S(1)}, s32[99,2]{0,1:T(2,128)}, u32[]{:S(2)}) %copy-start.5) | copy-done | bytes 816
  6.9 45.1 %shard_map.86 = (bf16[32,512]{1,0:T(8,128)(2,1)S(1)}, f32[32,256]{1,0:T(8,128)S(1)}) custom-call(bf16[32,512]{1,0:T(8,128)(2,1)S(1)} %copy-done.1, bf16[32,512]{1,0:T(8,128)(2,1)S(1)} %copy-done.2, bf16[32,512]{1,0:T(8,128)(2,1)S(1)} %copy-done.3, bf16[32,256]{1,0:T(8,128)(2,1)S(1)} %bitcast.2, bf16[99,128,128]{2,1,0:T(8,128)(2,1)S(1)} %copy-done, ...), custom_call_target="tpu_custom_call" | custom-call | flops 300000000 | bytes 6000000 | tf_op jit(solution)/shard_map/pallas_call | solution.py:229
  52.0 0.6 %copy.12 = bf16[32,512]{1,0:T(8,128)(2,1)} copy(bf16[32,512]{1,0:T(8,128)(2,1)S(1)} %get-tuple-element.4) | data formatting | bytes 65536
  52.6 0.6 %copy.13 = f32[32,256]{1,0:T(8,128)} copy(f32[32,256]{1,0:T(8,128)S(1)} %get-tuple-element.5) | data formatting | bytes 65536
Async XLA Ops:
  1.3 1.9 %copy-start = (bf16[99,128,128]{2,1,0:T(8,128)(2,1)S(1)}, bf16[99,128,128]{2,1,0:T(8,128)(2,1)}, u32[]{:S(2)}) copy-start(bf16[99,128,128]{2,1,0:T(8,128)(2,1)} %tiles_hbm.1) | copy-start | bytes 9732100
  3.2 0.8 %copy-start.1 = (bf16[32,512]{1,0:T(8,128)(2,1)S(1)}, bf16[32,512]{1,0:T(8,128)(2,1)}, u32[]{:S(2)}) copy-start(bf16[32,512]{1,0:T(8,128)(2,1)} %go_hbm.1) | copy-start | bytes 98308
  4.0 0.8 %copy-start.2 = (bf16[32,512]{1,0:T(8,128)(2,1)S(1)}, bf16[32,512]{1,0:T(8,128)(2,1)}, u32[]{:S(2)}) copy-start(bf16[32,512]{1,0:T(8,128)(2,1)} %pa_hbm.1) | copy-start | bytes 98308
  4.7 0.8 %copy-start.3 = (bf16[32,512]{1,0:T(8,128)(2,1)S(1)}, bf16[32,512]{1,0:T(8,128)(2,1)}, u32[]{:S(2)}) copy-start(bf16[32,512]{1,0:T(8,128)(2,1)} %agg_hbm.1) | copy-start | bytes 98308
  5.5 0.7 %copy-start.4 = (bf16[256,32]{0,1:T(8,128)(2,1)S(1)}, bf16[256,32]{0,1:T(8,128)(2,1)}, u32[]{:S(2)}) copy-start(bf16[256,32]{0,1:T(8,128)(2,1)} %param.10) | copy-start | bytes 49156
  6.2 0.7 %copy-start.5 = (s32[99,2]{0,1:T(2,128)S(1)}, s32[99,2]{0,1:T(2,128)}, u32[]{:S(2)}) copy-start(s32[99,2]{0,1:T(2,128)} %param.12) | copy-start | bytes 2380

commit v2 on v1

v2 whole, which is shorter than its diff:
```python
import jax
import jax.numpy as jnp
from jax import lax
from jax.experimental import pallas as pl
from jax.experimental.pallas import tpu as pltpu
from jax.sharding import PartitionSpec as P

YN, ZN, CORES, COLS = 8, 4, 2, 8
WN = ZN * CORES
ROWS = YN * WN
TILE = 128
BLOCKS = 4
FEAT = 32
NODES = BLOCKS * TILE
PARTS = 2
PART = BLOCKS // PARTS
PNODES = PART * TILE
SLOTS = 99
MESH = pl.DeviceIdType.MESH
SHEET = ((1, 2), (1, 1), (1, 3), (1, 0), (0, 2), (0, 1), (0, 3))


def kernel(
    go_hbm, pa_hbm, agg_hbm, wt_hbm, tiles_hbm, coords_hbm, count_hbm,
    fg_out, wg_out,
    go, pa, agg, wt, tiles, coords, count,
    masked, wpart, wrow, x, wl, ra, part, rb, final,
    in_sem, sent, w_recv, m_recv, z_recv, y_recv, s_recv, g_recv,
):
    row = lax.axis_index("row")
    col = lax.axis_index("col")
    y = row // WN
    w = row % WN
    z = w // CORES
    core = w % CORES
    sibling = row + 1 - 2 * core

    def col_of(dz, dx):
        return ((col // 4 + dz) % 2) * 4 + (col + dx) % 4

    def at_col(c):
        return {"row": row, "col": c}

    def at_row(r):
        return {"row": r, "col": col}

    def y_row(o):
        return ((y + o) % YN) * WN + w

    def w_row(o):
        return y * WN + (w + o) % WN

    def z_row(o):
        return y * WN + ((z + o) % ZN) * CORES + core

    loads = [
        pltpu.make_async_copy(src, dst, in_sem.at[n])
        for n, (src, dst) in enumerate((
            (go_hbm, go), (pa_hbm, pa), (wt_hbm, wt), (agg_hbm, agg),
            (coords_hbm, coords), (count_hbm, count), (tiles_hbm, tiles),
        ))
    ]
    for load in loads:
        load.start()

    barrier = pltpu.get_barrier_semaphore()
    for dz, dx in SHEET:
        pl.semaphore_signal(barrier, inc=1, device_id=at_col(col_of(dz, dx)), device_id_type=MESH)
    for o in range(1, YN):
        pl.semaphore_signal(barrier, inc=1, device_id=at_row(y_row(o)), device_id_type=MESH)
    for o in range(1, WN):
        pl.semaphore_signal(barrier, inc=1, device_id=at_row(w_row(o)), device_id_type=MESH)

    loads[0].wait()
    loads[1].wait()
    for h in range(PARTS):
        own_nodes = slice(h * PNODES, (h + 1) * PNODES)
        g = go[:, own_nodes]
        masked[h * COLS + col] = jnp.where(pa[:, own_nodes] > 0, g, jnp.zeros_like(g))
    loads[2].wait()
    wpart[col] = wt[:, pl.ds(pl.multiple_of((col // 4) * TILE, TILE), TILE)]

    pl.semaphore_wait(barrier, COLS - 1 + YN - 1 + WN - 1)

    def remote(src, dst, send, recv, to):
        return pltpu.make_async_remote_copy(
            src_ref=src, dst_ref=dst, send_sem=send, recv_sem=recv,
            device_id=to, device_id_type=MESH,
        )

    def send(src, dst, send_sem, recv_sem, to):
        remote(src, dst, send_sem, recv_sem, to).start()

    def arrived(ref, sem):
        pltpu.make_async_copy(ref, ref, sem).wait()

    y_sends = []

    others = COLS - 1
    for dz, dx in SHEET:
        peer = col_of(dz, dx)
        send(
            wt.at[:, pl.ds(pl.multiple_of((peer // 4) * TILE, TILE), TILE)],
            wpart.at[col], sent.at[0], w_recv.at[0], at_col(peer),
        )
    for h in range(PARTS):
        for dz, dx in SHEET:
            send(masked.at[h * COLS + col], masked.at[h * COLS + col], sent.at[1], m_recv.at[h],
                 at_col(col_of(dz, dx)))
    arrived(wpart.at[pl.ds(0, others)], w_recv.at[0])
    wrow[...] = wpart[...].reshape(COLS * FEAT, TILE).astype(jnp.float32).T
    own_w = wrow[pl.ds(pl.multiple_of((col % 4) * FEAT, FEAT), FEAT), :].astype(jnp.bfloat16)
    def part_of(r, h):
        return x.at[pl.ds(r * BLOCKS + h * PART, PART)]

    def to_y(step, d, h, k, far, r):
        send(part_of(r, h), part_of(r, h), sent.at[3], y_recv.at[far - 1, d, h],
             at_row(y_row((1 - 2 * step) * (far - k))))
        y_sends.append(far)

    def to_sibling(step, d, h, k, r):
        send(part_of(r, h), part_of(r, h), sent.at[4], s_recv.at[0], at_row(sibling))

    def source(step, d, k):
        return ((y - (1 - 2 * step) * k) % YN) * WN + ((z + d) % ZN) * CORES + core

    def masked_part(h):
        return masked[h * COLS:(h + 1) * COLS].reshape(COLS * FEAT, PNODES)

    for h in range(PARTS):
        arrived(masked.at[pl.ds(0, others)], m_recv.at[h])
        node_grad = jnp.dot(
            own_w, masked_part(h), preferred_element_type=jnp.float32
        ).astype(jnp.bfloat16)
        for b in range(PART):
            x[row * BLOCKS + h * PART + b] = node_grad[:, b * TILE:(b + 1) * TILE]
        to_y(0, 0, h, 0, 1, row)
        to_y(1, 0, h, 0, 1, row)
        for d in (1, 3, 2):
            send(part_of(row, h), part_of(row, h), sent.at[2], z_recv.at[ZN - d, h],
                 at_row(z_row(d)))
        to_sibling(0, 0, h, 0, row)

    loads[3].wait()
    wgrad = sum(
        lax.dot_general(
            agg[:, h * PNODES:(h + 1) * PNODES], masked_part(h),
            (((1,), (1,)), ((), ())), preferred_element_type=jnp.float32,
        )
        for h in range(PARTS)
    )
    for q in range(YN):
        piece = wgrad[(q // 2) * 8:(q // 2) * 8 + 8, (q % 2) * TILE:(q % 2 + 1) * TILE]
        wl[q] = piece
    ra[y] = wl[y]
    for o in range(1, YN):
        send(wl.at[(y + o) % YN], ra.at[y], sent.at[5], g_recv.at[0], at_row(y_row(o)))

    def from_z(d):
        r = z_row(d)
        for h in range(PARTS):
            arrived(part_of(r, h), z_recv.at[d, h])
            for far in (1, 2) if d == 2 else (1,):
                to_y(0, d, h, 0, far, r)
                to_y(1, d, h, 0, far, r)
            to_sibling(0, d, h, 0, r)

    def passed_on(step, d, k):
        if d == 2:
            return ((), (), (3,) if step == 0 else (3, 4), (), ())[k]
        return (k + 1,) if k < 3 or (k == 3 and last_leg(step, d)) else ()

    def last_leg(step, d):
        return step == (0 if d in (0, 1) else 1)

    def from_y(k, *ds):
        for d in ds:
            for h in range(PARTS):
                steps = [step for step in range(2) if k < YN // 2 or last_leg(step, d)]
                arrived(x.at[pl.ds(0, PART * len(steps))], y_recv.at[k - 1, d, h])
                for step in steps:
                    r = source(step, d, k)
                    for far in passed_on(step, d, k):
                        to_y(step, d, h, k, far, r)
                    to_sibling(step, d, h, k, r)

    from_y(1, 0)
    from_z(1)
    from_z(3)
    from_y(2, 0)

    arrived(ra.at[pl.ds(0, YN - 1)], g_recv.at[0])
    part[...] = jnp.sum(ra[...], axis=0)
    rb[w] = part[...]
    for o in range(1, WN):
        send(part, rb.at[w], sent.at[6], g_recv.at[1], at_row(w_row(o)))

    from_z(2)
    from_y(1, 1, 3)
    from_y(3, 0)
    from_y(1, 2)
    from_y(2, 1, 3)

    arrived(rb.at[pl.ds(0, WN - 1)], g_recv.at[1])
    final[y] = jnp.sum(rb[...], axis=0)
    for o in range(1, YN):
        send(final.at[y], final.at[y], sent.at[7], g_recv.at[2], at_row(y_row(o)))

    from_y(2, 2)
    from_y(4, 0)
    from_y(3, 1, 3, 2)
    from_y(4, 1, 3, 2)

    arrived(final.at[pl.ds(0, YN - 1)], g_recv.at[2])
    for q in range(YN):
        wg_out[(q // 2) * 8:(q // 2) * 8 + 8, (q % 2) * TILE:(q % 2 + 1) * TILE] = final[q]

    arrived(x.at[pl.ds(0, BLOCKS * ROWS // CORES)], s_recv.at[0])

    for load in loads[4:]:
        load.wait()
    in_use = count[0]
    first = row * BLOCKS
    group = 11
    total = jnp.zeros((BLOCKS * FEAT, TILE), jnp.float32)
    for g in range(0, SLOTS, group):
        pieces = []
        for t in range(g, g + group):
            here = x[coords[0, t]]
            j = jnp.where(t < in_use, coords[1, t] - first, -1)
            zero = jnp.zeros_like(here)
            pieces.append(jnp.concatenate(
                [jnp.where(j == b, here, zero) for b in range(BLOCKS)], axis=0))
        total += jnp.dot(
            jnp.concatenate(pieces, axis=1),
            tiles[g:g + group].reshape(group * TILE, TILE),
            preferred_element_type=jnp.float32,
        )
    for b in range(BLOCKS):
        fg_out[:, b * TILE:(b + 1) * TILE] = total[b * FEAT:(b + 1) * FEAT].astype(jnp.bfloat16)

    for n, ref in enumerate((
        wpart.at[pl.ds(0, others)], masked.at[pl.ds(0, PARTS * others)],
        x.at[pl.ds(0, (ZN - 1) * BLOCKS)], x.at[pl.ds(0, len(y_sends) * PART)],
        x.at[pl.ds(0, BLOCKS * ROWS // CORES)],
        wl.at[pl.ds(0, YN - 1)], rb.at[pl.ds(0, WN - 1)], final.at[pl.ds(0, YN - 1)],
    )):
        arrived(ref, sent.at[n])


def shards(grad_out, pre_act, aggregated, weight, tiles, tile_coords, tile_count):
    bf16, f32 = jnp.bfloat16, jnp.float32
    vmem, dma = pltpu.VMEM, pltpu.SemaphoreType.DMA
    return pl.pallas_call(
        kernel,
        out_shape=(
            jax.ShapeDtypeStruct((FEAT, NODES), bf16),
            jax.ShapeDtypeStruct((FEAT, COLS * FEAT), f32),
        ),
        in_specs=[pl.BlockSpec(memory_space=pl.ANY)] * 7,
        out_specs=(pl.BlockSpec(memory_space=vmem), pl.BlockSpec(memory_space=vmem)),
        scratch_shapes=[
            vmem((FEAT, NODES), bf16),
            vmem((FEAT, NODES), bf16),
            vmem((FEAT, NODES), bf16),
            vmem((FEAT, COLS * FEAT), bf16),
            vmem((SLOTS, TILE, TILE), bf16),
            pltpu.SMEM((2, SLOTS), jnp.int32),
            pltpu.SMEM((1,), jnp.int32),
            vmem((PARTS * COLS, FEAT, PNODES), bf16),
            vmem((COLS, FEAT, TILE), bf16),
            vmem((TILE, COLS * FEAT), f32),
            vmem((ROWS * BLOCKS, FEAT, TILE), bf16),
            vmem((YN, 8, TILE), f32),
            vmem((YN, 8, TILE), f32),
            vmem((8, TILE), f32),
            vmem((WN, 8, TILE), f32),
            vmem((YN, 8, TILE), f32),
            dma((7,)),
            dma((8,)), dma((1,)), dma((PARTS,)), dma((ZN, PARTS)), dma((YN // 2, ZN, PARTS)), dma((1,)), dma((3,)),
        ],
        compiler_params=pltpu.CompilerParams(
            collective_id=0, has_side_effects=True, vmem_limit_bytes=60 * 1024 * 1024,
        ),
        cost_estimate=pl.CostEstimate(flops=300_000_000, bytes_accessed=6_000_000, transcendentals=0),
    )(grad_out, pre_act, aggregated, weight.T, tiles, tile_coords.T, tile_count)


def solution(mesh):
    in_specs = (
        P("col", "row"),
        P("col", "row"),
        P("col", "row"),
        P(None, "col"),
        P("row", None, None),
        P("row", None),
        P("row"),
    )
    out_specs = (P("col", "row"), P("col", None))
    return jax.shard_map(shards, mesh=mesh, in_specs=in_specs, out_specs=out_specs, check_vma=False)
```

time: 53.7 us -> 47.1 us (0.88)
  local copies, waits for them, and re-layouts: 6.81 us -> 2.75 us
  Pallas kernels: 45.1 us -> 42.8 us
    unnamed x14 -> x2, local copies, waits for them, and re-layouts: 6.81 us -> 2.75 us
    pallas_call x1, Pallas kernels: 45.1 us -> 42.8 us  [shards(): pl.pallas_call(kernel, out_shape=(jax.ShapeDtypeStruct((FEAT, NODES), bf1...]
where the time goes in v2:
time: 47.1 us; the launch traced here: 46.9 us
  Pallas kernels  42.8 us (91%)
  local copies, waits for them, and re-layouts  2.75 us (6%)
  between operations  1.29 us (3%)
    pallas_call x1, Pallas kernels, shards(): pl.pallas_call(kernel, out_shape=(jax.ShapeDtypeStruct((FEAT, NODES), bf1...  42.8 us
    unnamed x2, local copies, waits for them, and re-layouts  2.75 us

profile of v2, /device:TPU:1, one launch (start us, length us, event | category | flops | bytes accessed | tf_op | source)
XLA Modules:
  0.0 46.9 jit_solution(16656319297291397307)
XLA Ops:
  1.3 42.8 %shard_map.86 = (bf16[32,512]{1,0:T(8,128)(2,1)}, f32[32,256]{1,0:T(8,128)}) custom-call(bf16[32,512]{1,0:T(8,128)(2,1)} %go_hbm.1, bf16[32,512]{1,0:T(8,128)(2,1)} %pa_hbm.1, bf16[32,512]{1,0:T(8,128)(2,1)} %agg_hbm.1, bf16[32,256]{1,0:T(8,128)(2,1)} %bitcast.2, bf16[99,128,128]{2,1,0:T(8,128)(2,1)} %tiles_hbm.1, s32[2,99]{1,0:T(2,128)} %bitcast.3, ...), custom_call_target="tpu_custom_call" | custom-call | flops 300000000 | bytes 6000000 | tf_op jit(solution)/shard_map/pallas_call | solution.py:254
  44.1 1.4 %copy.12 = bf16[32,512]{1,0:T(8,128)(2,1)} copy(bf16[32,512]{1,0:T(8,128)(2,1)} %get-tuple-element.4) | data formatting | bytes 65536
  45.5 1.4 %copy.13 = f32[32,256]{1,0:T(8,128)} copy(f32[32,256]{1,0:T(8,128)} %get-tuple-element.5) | data formatting | bytes 65536

commit v3 on v2

--- a/solution.py
+++ b/solution.py
@@ -94,7 +94,7 @@
     def arrived(ref, sem):
         pltpu.make_async_copy(ref, ref, sem).wait()
 
-    y_sends = []
+    y_sends, z_sends = [], []
 
     others = COLS - 1
     for dz, dx in SHEET:
@@ -118,6 +118,10 @@
              at_row(y_row((1 - 2 * step) * (far - k))))
         y_sends.append(far)
 
+    def to_z(d, h, r, sem):
+        send(part_of(r, h), part_of(r, h), sent.at[2], sem, at_row(z_row(d)))
+        z_sends.append(d)
+
     def to_sibling(step, d, h, k, r):
         send(part_of(r, h), part_of(r, h), sent.at[4], s_recv.at[0], at_row(sibling))
 
@@ -134,11 +138,11 @@
         ).astype(jnp.bfloat16)
         for b in range(PART):
             x[row * BLOCKS + h * PART + b] = node_grad[:, b * TILE:(b + 1) * TILE]
-        to_y(0, 0, h, 0, 1, row)
-        to_y(1, 0, h, 0, 1, row)
+        for far in (1, 2):
+            for step in range(2):
+                to_y(step, 0, h, 0, far, row)
         for d in (1, 3, 2):
-            send(part_of(row, h), part_of(row, h), sent.at[2], z_recv.at[ZN - d, h],
-                 at_row(z_row(d)))
+            to_z(d, h, row, z_recv.at[ZN - d, h])
         to_sibling(0, 0, h, 0, row)
 
     loads[3].wait()
@@ -166,9 +170,9 @@
             to_sibling(0, d, h, 0, r)
 
     def passed_on(step, d, k):
-        if d == 2:
-            return ((), (), (3,) if step == 0 else (3, 4), (), ())[k]
-        return (k + 1,) if k < 3 or (k == 3 and last_leg(step, d)) else ()
+        if d in (1, 3):
+            return (2,) if k == 1 else ()
+        return () if k != 2 else (3, 4) if last_leg(step, d) else (3,)
 
     def last_leg(step, d):
         return step == (0 if d in (0, 1) else 1)
@@ -182,12 +186,15 @@
                     r = source(step, d, k)
                     for far in passed_on(step, d, k):
                         to_y(step, d, h, k, far, r)
+                    if d == 0 and k > 2:
+                        for o in (1, 3):
+                            to_z(o, h, r, y_recv.at[k - 1, ZN - o, h])
                     to_sibling(step, d, h, k, r)
 
     from_y(1, 0)
+    from_y(2, 0)
     from_z(1)
     from_z(3)
-    from_y(2, 0)
 
     arrived(ra.at[pl.ds(0, YN - 1)], g_recv.at[0])
     part[...] = jnp.sum(ra[...], axis=0)
@@ -195,21 +202,23 @@
     for o in range(1, WN):
         send(part, rb.at[w], sent.at[6], g_recv.at[1], at_row(w_row(o)))
 
+    from_y(3, 0)
     from_z(2)
     from_y(1, 1, 3)
-    from_y(3, 0)
+    from_y(4, 0)
     from_y(1, 2)
-    from_y(2, 1, 3)
+    from_y(2, 2)
 
     arrived(rb.at[pl.ds(0, WN - 1)], g_recv.at[1])
     final[y] = jnp.sum(rb[...], axis=0)
     for o in range(1, YN):
         send(final.at[y], final.at[y], sent.at[7], g_recv.at[2], at_row(y_row(o)))
 
-    from_y(2, 2)
-    from_y(4, 0)
-    from_y(3, 1, 3, 2)
-    from_y(4, 1, 3, 2)
+    from_y(2, 1, 3)
+    from_y(3, 1, 3)
+    from_y(4, 1, 3)
+    from_y(3, 2)
+    from_y(4, 2)
 
     arrived(final.at[pl.ds(0, YN - 1)], g_recv.at[2])
     for q in range(YN):
@@ -241,7 +250,7 @@
 
     for n, ref in enumerate((
         wpart.at[pl.ds(0, others)], masked.at[pl.ds(0, PARTS * others)],
-        x.at[pl.ds(0, (ZN - 1) * BLOCKS)], x.at[pl.ds(0, len(y_sends) * PART)],
+        x.at[pl.ds(0, len(z_sends) * PART)], x.at[pl.ds(0, len(y_sends) * PART)],
         x.at[pl.ds(0, BLOCKS * ROWS // CORES)],
         wl.at[pl.ds(0, YN - 1)], rb.at[pl.ds(0, WN - 1)], final.at[pl.ds(0, YN - 1)],
     )):

time: 47.1 us -> 46.2 us (0.981)
  Pallas kernels: 42.8 us -> 41.9 us
    pallas_call x1, Pallas kernels: 42.8 us -> 41.9 us  [shards(): pl.pallas_call(kernel, out_shape=(jax.ShapeDtypeStruct((FEAT, NODES), bf1...]
where the time goes in v3:
time: 46.2 us; the launch traced here: 45.9 us
  Pallas kernels  41.9 us (91%)
  local copies, waits for them, and re-layouts  2.75 us (6%)
  between operations  1.29 us (3%)
    pallas_call x1, Pallas kernels, shards(): pl.pallas_call(kernel, out_shape=(jax.ShapeDtypeStruct((FEAT, NODES), bf1...  41.9 us
    unnamed x2, local copies, waits for them, and re-layouts  2.75 us

profile of v3, /device:TPU:1, one launch (start us, length us, event | category | flops | bytes accessed | tf_op | source)
XLA Modules:
  0.0 45.9 jit_solution(3667070523230734352)
XLA Ops:
  1.3 41.9 %shard_map.86 = (bf16[32,512]{1,0:T(8,128)(2,1)}, f32[32,256]{1,0:T(8,128)}) custom-call(bf16[32,512]{1,0:T(8,128)(2,1)} %go_hbm.1, bf16[32,512]{1,0:T(8,128)(2,1)} %pa_hbm.1, bf16[32,512]{1,0:T(8,128)(2,1)} %agg_hbm.1, bf16[32,256]{1,0:T(8,128)(2,1)} %bitcast.2, bf16[99,128,128]{2,1,0:T(8,128)(2,1)} %tiles_hbm.1, s32[2,99]{1,0:T(2,128)} %bitcast.3, ...), custom_call_target="tpu_custom_call" | custom-call | flops 300000000 | bytes 6000000 | tf_op jit(solution)/shard_map/pallas_call | solution.py:263
  43.2 1.4 %copy.12 = bf16[32,512]{1,0:T(8,128)(2,1)} copy(bf16[32,512]{1,0:T(8,128)(2,1)} %get-tuple-element.4) | data formatting | bytes 65536
  44.6 1.4 %copy.13 = f32[32,256]{1,0:T(8,128)} copy(f32[32,256]{1,0:T(8,128)} %get-tuple-element.5) | data formatting | bytes 65536

commit v4 on v3

--- a/solution.py
+++ b/solution.py
@@ -263,8 +263,8 @@
     return pl.pallas_call(
         kernel,
         out_shape=(
-            jax.ShapeDtypeStruct((FEAT, NODES), bf16),
-            jax.ShapeDtypeStruct((FEAT, COLS * FEAT), f32),
+            vmem((FEAT, NODES), bf16),
+            vmem((FEAT, COLS * FEAT), f32),
         ),
         in_specs=[pl.BlockSpec(memory_space=pl.ANY)] * 7,
         out_specs=(pl.BlockSpec(memory_space=vmem), pl.BlockSpec(memory_space=vmem)),
@@ -289,7 +289,7 @@
             dma((8,)), dma((1,)), dma((PARTS,)), dma((ZN, PARTS)), dma((YN // 2, ZN, PARTS)), dma((1,)), dma((3,)),
         ],
         compiler_params=pltpu.CompilerParams(
-            collective_id=0, has_side_effects=True, vmem_limit_bytes=60 * 1024 * 1024,
+            collective_id=0, has_side_effects=True, vmem_limit_bytes=55168 * 1024,
         ),
         cost_estimate=pl.CostEstimate(flops=300_000_000, bytes_accessed=6_000_000, transcendentals=0),
     )(grad_out, pre_act, aggregated, weight.T, tiles, tile_coords.T, tile_count)

time: 46.2 us -> 43.9 us (0.950)
  local copies, waits for them, and re-layouts: 2.75 us -> 1.23 us
  Pallas kernels: 41.9 us -> 41.3 us
    unnamed x2, local copies, waits for them, and re-layouts: 2.75 us -> 1.23 us
    pallas_call x1, Pallas kernels: 41.9 us -> 41.3 us  [shards(): pl.pallas_call(kernel, out_shape=(vmem((FEAT, NODES), bf16), vmem((FEAT,...]
where the time goes in v4:
time: 43.9 us; the launch traced here: 43.8 us
  Pallas kernels  41.3 us (94%)
  between operations  1.29 us (3%)
  local copies, waits for them, and re-layouts  1.23 us (3%)
    pallas_call x1, Pallas kernels, shards(): pl.pallas_call(kernel, out_shape=(vmem((FEAT, NODES), bf16), vmem((FEAT,...  41.3 us
    unnamed x2, local copies, waits for them, and re-layouts  1.23 us

profile of v4, /device:TPU:1, one launch (start us, length us, event | category | flops | bytes accessed | tf_op | source)
XLA Modules:
  0.0 43.8 jit_solution(15764552258310537518)
XLA Ops:
  1.3 41.3 %shard_map.86 = (bf16[32,512]{1,0:T(8,128)(2,1)S(1)}, f32[32,256]{1,0:T(8,128)S(1)}) custom-call(bf16[32,512]{1,0:T(8,128)(2,1)} %go_hbm.1, bf16[32,512]{1,0:T(8,128)(2,1)} %pa_hbm.1, bf16[32,512]{1,0:T(8,128)(2,1)} %agg_hbm.1, bf16[32,256]{1,0:T(8,128)(2,1)} %bitcast.2, bf16[99,128,128]{2,1,0:T(8,128)(2,1)} %tiles_hbm.1, s32[2,99]{1,0:T(2,128)} %bitcast.3, ...), custom_call_target="tpu_custom_call" | custom-call | flops 300000000 | bytes 6000000 | tf_op jit(solution)/shard_map/pallas_call | solution.py:263
  42.6 0.6 %copy.11 = bf16[32,512]{1,0:T(8,128)(2,1)} copy(bf16[32,512]{1,0:T(8,128)(2,1)S(1)} %get-tuple-element.2) | data formatting | bytes 65536
  43.2 0.6 %copy.12 = f32[32,256]{1,0:T(8,128)} copy(f32[32,256]{1,0:T(8,128)S(1)} %get-tuple-element.3) | data formatting | bytes 65536

commit v5 on v4

--- a/solution.py
+++ b/solution.py
@@ -12,7 +12,7 @@
 BLOCKS = 4
 FEAT = 32
 NODES = BLOCKS * TILE
-PARTS = 2
+PARTS = 1
 PART = BLOCKS // PARTS
 PNODES = PART * TILE
 SLOTS = 99
@@ -193,26 +193,26 @@
 
     from_y(1, 0)
     from_y(2, 0)
-    from_z(1)
-    from_z(3)
-
     arrived(ra.at[pl.ds(0, YN - 1)], g_recv.at[0])
     part[...] = jnp.sum(ra[...], axis=0)
     rb[w] = part[...]
     for o in range(1, WN):
         send(part, rb.at[w], sent.at[6], g_recv.at[1], at_row(w_row(o)))
 
+    from_z(1)
+    from_z(3)
+
     from_y(3, 0)
     from_z(2)
     from_y(1, 1, 3)
-    from_y(4, 0)
-    from_y(1, 2)
-    from_y(2, 2)
-
     arrived(rb.at[pl.ds(0, WN - 1)], g_recv.at[1])
     final[y] = jnp.sum(rb[...], axis=0)
     for o in range(1, YN):
         send(final.at[y], final.at[y], sent.at[7], g_recv.at[2], at_row(y_row(o)))
+
+    from_y(4, 0)
+    from_y(1, 2)
+    from_y(2, 2)
 
     from_y(2, 1, 3)
     from_y(3, 1, 3)

time: 43.9 us -> 42.9 us (0.977)
  Pallas kernels: 41.3 us -> 40.2 us
    pallas_call x1, Pallas kernels: 41.3 us -> 40.2 us  [shards(): pl.pallas_call(kernel, out_shape=(vmem((FEAT, NODES), bf16), vmem((FEAT,...]
where the time goes in v5:
time: 42.9 us; the launch traced here: 42.7 us
  Pallas kernels  40.2 us (94%)
  between operations  1.29 us (3%)
  local copies, waits for them, and re-layouts  1.23 us (3%)
    pallas_call x1, Pallas kernels, shards(): pl.pallas_call(kernel, out_shape=(vmem((FEAT, NODES), bf16), vmem((FEAT,...  40.2 us
    unnamed x2, local copies, waits for them, and re-layouts  1.23 us

profile of v5, /device:TPU:1, one launch (start us, length us, event | category | flops | bytes accessed | tf_op | source)
XLA Modules:
  0.0 42.7 jit_solution(8306088315078404969)
XLA Ops:
  1.3 40.2 %shard_map.86 = (bf16[32,512]{1,0:T(8,128)(2,1)S(1)}, f32[32,256]{1,0:T(8,128)S(1)}) custom-call(bf16[32,512]{1,0:T(8,128)(2,1)} %go_hbm.1, bf16[32,512]{1,0:T(8,128)(2,1)} %pa_hbm.1, bf16[32,512]{1,0:T(8,128)(2,1)} %agg_hbm.1, bf16[32,256]{1,0:T(8,128)(2,1)} %bitcast.2, bf16[99,128,128]{2,1,0:T(8,128)(2,1)} %tiles_hbm.1, s32[2,99]{1,0:T(2,128)} %bitcast.3, ...), custom_call_target="tpu_custom_call" | custom-call | flops 300000000 | bytes 6000000 | tf_op jit(solution)/shard_map/pallas_call | solution.py:263
  41.5 0.6 %copy.11 = bf16[32,512]{1,0:T(8,128)(2,1)} copy(bf16[32,512]{1,0:T(8,128)(2,1)S(1)} %get-tuple-element.2) | data formatting | bytes 65536
  42.1 0.6 %copy.12 = f32[32,256]{1,0:T(8,128)} copy(f32[32,256]{1,0:T(8,128)S(1)} %get-tuple-element.3) | data formatting | bytes 65536

commit v6 on v5

--- a/solution.py
+++ b/solution.py
@@ -141,7 +141,7 @@
         for far in (1, 2):
             for step in range(2):
                 to_y(step, 0, h, 0, far, row)
-        for d in (1, 3, 2):
+        for d in (2, 1, 3):
             to_z(d, h, row, z_recv.at[ZN - d, h])
         to_sibling(0, 0, h, 0, row)
 
@@ -202,8 +202,8 @@
     from_z(1)
     from_z(3)
 
+    from_z(2)
     from_y(3, 0)
-    from_z(2)
     from_y(1, 1, 3)
     arrived(rb.at[pl.ds(0, WN - 1)], g_recv.at[1])
     final[y] = jnp.sum(rb[...], axis=0)

time: 42.9 us -> 42.9 us (level)
  no operation moved by 1% of the time
where the time goes in v6:
time: 42.9 us; the launch traced here: 42.8 us
  Pallas kernels  40.3 us (94%)
  between operations  1.29 us (3%)
  local copies, waits for them, and re-layouts  1.23 us (3%)
    pallas_call x1, Pallas kernels, shards(): pl.pallas_call(kernel, out_shape=(vmem((FEAT, NODES), bf16), vmem((FEAT,...  40.3 us
    unnamed x2, local copies, waits for them, and re-layouts  1.23 us

profile of v6, /device:TPU:1, one launch (start us, length us, event | category | flops | bytes accessed | tf_op | source)
XLA Modules:
  0.0 42.8 jit_solution(16697922932226564054)
XLA Ops:
  1.3 40.3 %shard_map.86 = (bf16[32,512]{1,0:T(8,128)(2,1)S(1)}, f32[32,256]{1,0:T(8,128)S(1)}) custom-call(bf16[32,512]{1,0:T(8,128)(2,1)} %go_hbm.1, bf16[32,512]{1,0:T(8,128)(2,1)} %pa_hbm.1, bf16[32,512]{1,0:T(8,128)(2,1)} %agg_hbm.1, bf16[32,256]{1,0:T(8,128)(2,1)} %bitcast.2, bf16[99,128,128]{2,1,0:T(8,128)(2,1)} %tiles_hbm.1, s32[2,99]{1,0:T(2,128)} %bitcast.3, ...), custom_call_target="tpu_custom_call" | custom-call | flops 300000000 | bytes 6000000 | tf_op jit(solution)/shard_map/pallas_call | solution.py:263
  41.5 0.6 %copy.11 = bf16[32,512]{1,0:T(8,128)(2,1)} copy(bf16[32,512]{1,0:T(8,128)(2,1)S(1)} %get-tuple-element.2) | data formatting | bytes 65536
  42.2 0.6 %copy.12 = f32[32,256]{1,0:T(8,128)} copy(f32[32,256]{1,0:T(8,128)S(1)} %get-tuple-element.3) | data formatting | bytes 65536

commit v7 on v6

--- a/solution.py
+++ b/solution.py
@@ -202,8 +202,8 @@
     from_z(1)
     from_z(3)
 
+    from_y(3, 0)
     from_z(2)
-    from_y(3, 0)
     from_y(1, 1, 3)
     arrived(rb.at[pl.ds(0, WN - 1)], g_recv.at[1])
     final[y] = jnp.sum(rb[...], axis=0)

time: 42.9 us -> 42.9 us (level)
  no operation moved by 1% of the time
where the time goes in v7:
time: 42.9 us; the launch traced here: 42.8 us
  Pallas kernels  40.3 us (94%)
  between operations  1.29 us (3%)
  local copies, waits for them, and re-layouts  1.23 us (3%)
    pallas_call x1, Pallas kernels, shards(): pl.pallas_call(kernel, out_shape=(vmem((FEAT, NODES), bf16), vmem((FEAT,...  40.3 us
    unnamed x2, local copies, waits for them, and re-layouts  1.23 us

profile of v7, /device:TPU:1, one launch (start us, length us, event | category | flops | bytes accessed | tf_op | source)
XLA Modules:
  0.0 42.8 jit_solution(12133251206621091564)
XLA Ops:
  1.3 40.3 %shard_map.86 = (bf16[32,512]{1,0:T(8,128)(2,1)S(1)}, f32[32,256]{1,0:T(8,128)S(1)}) custom-call(bf16[32,512]{1,0:T(8,128)(2,1)} %go_hbm.1, bf16[32,512]{1,0:T(8,128)(2,1)} %pa_hbm.1, bf16[32,512]{1,0:T(8,128)(2,1)} %agg_hbm.1, bf16[32,256]{1,0:T(8,128)(2,1)} %bitcast.2, bf16[99,128,128]{2,1,0:T(8,128)(2,1)} %tiles_hbm.1, s32[2,99]{1,0:T(2,128)} %bitcast.3, ...), custom_call_target="tpu_custom_call" | custom-call | flops 300000000 | bytes 6000000 | tf_op jit(solution)/shard_map/pallas_call | solution.py:263
  41.6 0.6 %copy.11 = bf16[32,512]{1,0:T(8,128)(2,1)} copy(bf16[32,512]{1,0:T(8,128)(2,1)S(1)} %get-tuple-element.2) | data formatting | bytes 65536
  42.2 0.6 %copy.12 = f32[32,256]{1,0:T(8,128)} copy(f32[32,256]{1,0:T(8,128)S(1)} %get-tuple-element.3) | data formatting | bytes 65536

commit v8 on v4

--- a/solution.py
+++ b/solution.py
@@ -12,7 +12,7 @@
 BLOCKS = 4
 FEAT = 32
 NODES = BLOCKS * TILE
-PARTS = 2
+PARTS = 1
 PART = BLOCKS // PARTS
 PNODES = PART * TILE
 SLOTS = 99

time: 43.9 us -> 43 us (0.979)
  Pallas kernels: 41.3 us -> 40.4 us
    pallas_call x1, Pallas kernels: 41.3 us -> 40.4 us  [shards(): pl.pallas_call(kernel, out_shape=(vmem((FEAT, NODES), bf16), vmem((FEAT,...]
where the time goes in v8:
time: 43 us; the launch traced here: 42.9 us
  Pallas kernels  40.4 us (94%)
  between operations  1.29 us (3%)
  local copies, waits for them, and re-layouts  1.23 us (3%)
    pallas_call x1, Pallas kernels, shards(): pl.pallas_call(kernel, out_shape=(vmem((FEAT, NODES), bf16), vmem((FEAT,...  40.4 us
    unnamed x2, local copies, waits for them, and re-layouts  1.23 us

profile of v8, /device:TPU:1, one launch (start us, length us, event | category | flops | bytes accessed | tf_op | source)
XLA Modules:
  0.0 42.9 jit_solution(15082074460119629061)
XLA Ops:
  1.3 40.4 %shard_map.86 = (bf16[32,512]{1,0:T(8,128)(2,1)S(1)}, f32[32,256]{1,0:T(8,128)S(1)}) custom-call(bf16[32,512]{1,0:T(8,128)(2,1)} %go_hbm.1, bf16[32,512]{1,0:T(8,128)(2,1)} %pa_hbm.1, bf16[32,512]{1,0:T(8,128)(2,1)} %agg_hbm.1, bf16[32,256]{1,0:T(8,128)(2,1)} %bitcast.2, bf16[99,128,128]{2,1,0:T(8,128)(2,1)} %tiles_hbm.1, s32[2,99]{1,0:T(2,128)} %bitcast.3, ...), custom_call_target="tpu_custom_call" | custom-call | flops 300000000 | bytes 6000000 | tf_op jit(solution)/shard_map/pallas_call | solution.py:263
  41.7 0.6 %copy.11 = bf16[32,512]{1,0:T(8,128)(2,1)} copy(bf16[32,512]{1,0:T(8,128)(2,1)S(1)} %get-tuple-element.2) | data formatting | bytes 65536
  42.3 0.6 %copy.12 = f32[32,256]{1,0:T(8,128)} copy(f32[32,256]{1,0:T(8,128)S(1)} %get-tuple-element.3) | data formatting | bytes 65536
